TPU v7x, 32 devices: a whole 2x2x4 slice. The times are simulated.
32 devices in a mesh: groups: 2 (over x), region: 16 (over z, y, core).
Axes of the slice: x: 2, y: 2, z: 4, core: 2. Of those that a mesh axis runs over, the one named last changes fastest.
Arguments:
- environment: bfloat16 [160, 96, 3264], P(('groups', 'region')), parts along dimension 0, may hold values from -6 to 6
- site_tensors: bfloat16 [160, 1, 4, 96, 96], P(('groups', 'region')), parts along dimension 0, may hold values from -0.625 to 0.625
- operator_blocks: bfloat16 [34, 4, 34], replicated, may hold values from -0.5 to 0.5
- join_in: int32 [80, 4], P('groups'), parts along dimension 0, may hold values from -1 to 39, as said below
- block_sizes: int32 [80], P('groups'), parts along dimension 0, may hold values from 48 to 96
Outputs:
- advanced: bfloat16 [160, 96, 3264], P(('groups', 'region')), parts along dimension 0
There are 2 independent parts, one for each index of `groups`. A program takes and returns all parts, laid end to end along the dimension named above; an argument that names none is the same for every part. Nothing has to cross between parts.
Inputs may be any that keep to these rules, and one draw needn't show every extreme that they name: Sectors are ordered by particle number, then spin, with at most 5 sectors to one particle number; a site adds 0 to 2 particles, so join_in[b, 0] = b and every other entry is -1 or lies between b - 2 * 5 + 1 and b - 1.
All inputs are finite; a program needn't handle non-finite values.
Results may differ from a plain program's by a relative error of at most 0.0058.
Values may be sent and summed in bfloat16 or wider, within the bound.
No kernel may reach another device: no remote copies, remote signals or barrier semaphores. Data moves between devices by JAX's collectives and lax.ppermute only.
A program may use at most 128 MiB of HBM per device.

v0:
```python
import functools

import jax
import jax.numpy as jnp
from jax import lax
from jax.experimental import pallas as pl
from jax.experimental.pallas import tpu as pltpu
from jax.sharding import PartitionSpec as P

OWN = 8
LANES = 128
CHUNK = 544
STEP = 16
GROUP = 4


def shifted(value, axis, steps):
    count = lax.axis_size(axis)
    return lax.ppermute(value, axis, [(source, (source + steps) % count) for source in range(count)])


def to_next(value, axis):
    count = lax.axis_size(axis)
    pairs = [(source, source + 1) for source in range(count) if source % OWN < OWN - 1]
    return lax.ppermute(value, axis, pairs)


def to_second(value, from_last, axis):
    count = lax.axis_size(axis)
    middle = OWN // 2
    regions = range(0, count, OWN)
    relay = lax.ppermute(value, axis, [(r + middle - 2, r) for r in regions])
    steps = [(0, middle)] + [(o, o + 1) for o in range(1, OWN - 1) if o != middle - 1]
    sent = jnp.where(lax.axis_index(axis) % OWN == 0, relay, from_last)
    return lax.ppermute(sent, axis, [(r + a, r + b) for r in regions for a, b in steps])


def tied(value, *after):
    return lax.optimization_barrier((value, after))[0]


def more_units(size, low, tile):
    units = (size > low).astype(jnp.int32)
    for start in range(low + STEP, tile, STEP):
        units += (size > start).astype(jnp.int32)
    return units


def base_copies(parts, low, env_ref, base_refs, sems):
    copies = []
    for number, (part, ref) in enumerate(zip(parts, base_refs)):
        source = env_ref.at[part.start : part.stop, :low]
        copies.append(pltpu.make_async_copy(source, ref, sems.at[number]))
    for copy in copies:
        copy.start()
    return copies


def pool_kernel(slots, parts, low, tile, owner, sizes, env_ref, *refs):
    *base_refs, out_ref, sems = refs
    copies = base_copies(parts, low, env_ref, base_refs, sems)
    at = jnp.int32(0)
    for slot in reversed(range(slots)):
        units = more_units(sizes[owner[0] * slots + slot], low, tile)
        for unit in range((tile - low) // STEP):

            @pl.when(unit < units)
            def _():
                out_ref[at + unit] = env_ref[slot, low + unit * STEP : low + (unit + 1) * STEP, :]

        at += units
    for copy in copies:
        copy.wait()


def pooled(owner, sizes, environment, parts, low):
    slots, tile, wide = environment.shape
    rest = tile - low
    outs = [jax.ShapeDtypeStruct((len(part), low, wide), environment.dtype) for part in parts]
    pool = jax.ShapeDtypeStruct((slots * rest // STEP, STEP, wide), environment.dtype)
    *bases, pool = pl.pallas_call(
        functools.partial(pool_kernel, slots, parts, low, tile),
        out_shape=outs + [pool],
        grid_spec=pltpu.PrefetchScalarGridSpec(
            num_scalar_prefetch=2,
            grid=(1,),
            in_specs=[pl.BlockSpec((slots, tile, wide), lambda i, *_: (0, 0, 0), pipeline_mode=pl.Buffered(1))],
            out_specs=[pl.BlockSpec(memory_space=pl.ANY)] * len(parts)
            + [pl.BlockSpec(pool.shape, lambda i, *_: (0, 0, 0))],
            scratch_shapes=[pltpu.SemaphoreType.DMA((len(parts),))],
        ),
        compiler_params=pltpu.CompilerParams(vmem_limit_bytes=60 * 1024 * 1024),
        cost_estimate=pl.CostEstimate(flops=1000, bytes_accessed=1024, transcendentals=0),
    )(owner, sizes, environment)
    return bases, pool


def pool_shifted(total, pool):
    def branch(units):
        def run(value):
            if units == 0:
                return value
            if units == value.shape[0]:
                return shifted(value, "region", OWN)
            return lax.dynamic_update_slice(value, shifted(value[:units], "region", OWN), (0, 0, 0))

        return run

    return lax.switch(total, [branch(units) for units in range(pool.shape[0] + 1)], pool)


def stage_kernel(first, last, wanted, hops, slots, owner, join, sizes, *refs):
    count = len(wanted)
    listed = [(hop, part[i], ref, i) for ref, (hop, part) in enumerate(wanted) for i in range(len(part))]
    block_refs, refs = refs[:count], refs[count:]
    pool_refs, refs = refs[:hops], refs[hops:]
    count = 0
    site_ref, ops_ref = refs[count : count + 2]
    acc_in = None if first else refs[count + 2]
    result, slab, mix, yf, vb, *rest = refs[count + 2 + (not first) :]
    tile = site_ref.shape[-1]
    states = ops_ref.shape[0]
    chans = block_refs[0].shape[-1] // tile
    span = GROUP * chans
    b = pl.program_id(0)
    base = owner[0] * slots
    acc = rest[0] if last else result.at[b]

    @pl.when(b == 0)
    def _():
        low = block_refs[0].shape[1]

        def spread(place, rows, value):
            pad = jnp.zeros((rows.stop - rows.start, LANES - tile), jnp.bfloat16)
            for w in range(chans):
                piece = value[:, w * tile : (w + 1) * tile]
                slab[place, rows, w * LANES : (w + 1) * LANES] = jnp.concatenate([piece, pad], axis=1)

        for place, (hop, slot, ref, index) in enumerate(listed):
            spread(place, slice(0, low), block_refs[ref][index])
            holder = jnp.maximum(owner[0] - hop, 0) * slots
            at = jnp.int32(0)
            for other in range(slot + 1, slots):
                at += more_units(sizes[holder + other], low, tile)
            units = more_units(sizes[holder + slot], low, tile)
            for unit in range((tile - low) // STEP):
                rows = slice(low + unit * STEP, low + (unit + 1) * STEP)

                @pl.when(unit < units)
                def _():
                    spread(place, rows, pool_refs[hop][at + unit])

                @pl.when(unit >= units)
                def _():
                    slab[place, rows, :] = jnp.zeros((STEP, chans * LANES), jnp.bfloat16)

        row = lax.broadcasted_iota(jnp.int32, (span, chans), 0)
        channel = lax.broadcasted_iota(jnp.int32, (span, chans), 1)
        pick = jnp.zeros((span, chans), jnp.bfloat16)
        for g in range(GROUP):
            pick += (row == channel + g * chans).astype(jnp.float32).astype(jnp.bfloat16)
        left = lax.broadcasted_iota(jnp.int32, (span, span), 0)
        right = lax.broadcasted_iota(jnp.int32, (span, span), 1)
        same = jnp.zeros((span, span), jnp.bool_)
        for g in range(GROUP):
            low_end, high_end = g * chans, (g + 1) * chans
            same |= (left >= low_end) & (left < high_end) & (right >= low_end) & (right < high_end)
        for q in range(states):
            spread_rows = jnp.dot(pick, ops_ref[q], preferred_element_type=jnp.float32).astype(jnp.bfloat16)
            both = lax.dot_general(spread_rows, pick, (((1,), (1,)), ((), ())), preferred_element_type=jnp.float32)
            mix[q] = jnp.where(same, both, 0.0).astype(jnp.bfloat16)

    acc[...] = jnp.zeros(acc.shape, jnp.float32) if first else acc_in[b]
    own_size = sizes[base + b]
    for q in range(states):
        a = join[base + b, q]
        place = jnp.int32(-1)
        for at, (hop, slot, _, _) in enumerate(listed):
            place = jnp.where(a - base == slot - hop * slots, at, place)

        @pl.when((a >= 0) & (place >= 0))
        def _():
            x = lax.broadcasted_iota(jnp.int32, (tile, tile), 0)
            u = lax.broadcasted_iota(jnp.int32, (tile, tile), 1)
            keep = (x < sizes[jnp.maximum(a, 0)]) & (u < own_size)
            g32 = jnp.where(keep, site_ref[0, 0, q].astype(jnp.float32), 0.0)
            gt = g32.T.astype(jnp.bfloat16)
            gy = jnp.concatenate([g32, jnp.zeros((tile, LANES - tile), jnp.float32)], axis=1)
            gy = jnp.concatenate([gy, jnp.zeros((LANES - tile, LANES), jnp.float32)], axis=0).astype(jnp.bfloat16)
            for c in range(0, chans, 2):
                y = jnp.dot(gt, slab[place, :, c * LANES : (c + 2) * LANES], preferred_element_type=jnp.float32)
                yf[pl.ds(c, tile, stride=chans), :] = y[:, :LANES]
                yf[pl.ds(c + 1, tile, stride=chans), :] = y[:, LANES:]
            for g in range(0, tile // GROUP, 2):
                one, two = (slice((g + k) * span, (g + k + 1) * span) for k in range(2))
                rhs = jnp.concatenate([yf[one, :].astype(jnp.bfloat16), yf[two, :].astype(jnp.bfloat16)], axis=1)
                v = jnp.dot(mix[q], rhs, preferred_element_type=jnp.float32)
                v = jnp.concatenate([v[:, :LANES], v[:, LANES:]], axis=0).astype(jnp.bfloat16)
                vb[g * span : (g + 2) * span, :] = v
            for g in range(0, tile * chans, CHUNK):
                some = slice(g, g + CHUNK)
                acc[some, :] += jnp.dot(vb[some, :], gy, preferred_element_type=jnp.float32)

    if last:
        for w in range(chans):
            done = acc[pl.ds(w, tile, stride=chans), :].astype(jnp.bfloat16)
            result[0, :, w * tile : (w + 1) * tile] = done[:, :tile]


def stage(owner, join, sizes, wanted, blocks, pools, tensors, ops, acc, last):
    slots, _, states, tile, _ = tensors.shape
    wide = blocks[0].shape[-1]
    chans = wide // tile
    first = acc is None
    full = tile * chans

    def whole(a):
        return pl.BlockSpec(a.shape, lambda b, *_: (0,) * a.ndim, pipeline_mode=pl.Buffered(1))

    def one(a):
        return pl.BlockSpec((1,) + a.shape[1:], lambda b, *_: (b,) + (0,) * (a.ndim - 1))

    args = list(blocks) + list(pools) + [tensors, ops]
    specs = [whole(a) for a in blocks] + [whole(a) for a in pools] + [one(tensors), whole(ops)]
    if not first:
        args.append(acc)
        specs.append(pl.BlockSpec(memory_space=pltpu.VMEM))
    if last:
        out = jax.ShapeDtypeStruct((slots, tile, wide), jnp.bfloat16)
    else:
        out = pltpu.VMEM((slots, full, LANES), jnp.float32)
    scratch = [
        pltpu.VMEM((sum(len(part) for _, part in wanted), tile, chans * LANES), jnp.bfloat16),
        pltpu.VMEM((states, GROUP * chans, GROUP * chans), jnp.bfloat16),
        pltpu.VMEM((full, LANES), jnp.float32),
        pltpu.VMEM((full, LANES), jnp.bfloat16),
    ]
    if last:
        scratch.append(pltpu.VMEM((full, LANES), jnp.float32))
    aliases = {} if first or last else {len(args) + 2: 0}
    return pl.pallas_call(
        functools.partial(stage_kernel, first, last, tuple(wanted), len(pools), slots),
        out_shape=out,
        grid_spec=pltpu.PrefetchScalarGridSpec(
            num_scalar_prefetch=3, grid=(slots,), in_specs=specs, out_specs=one(out) if last else pl.BlockSpec(memory_space=pltpu.VMEM), scratch_shapes=scratch
        ),
        input_output_aliases=aliases,
        compiler_params=pltpu.CompilerParams(vmem_limit_bytes=32 * 1024 * 1024),
        cost_estimate=pl.CostEstimate(flops=10**10, bytes_accessed=2**20, transcendentals=0),
    )(owner, join, sizes, *args)


def per_device(environment, site_tensors, operator_blocks, join_in, block_sizes):
    slots, tile, _ = environment.shape
    chans = operator_blocks.shape[0]
    owner = (lax.axis_index("region") % OWN).astype(jnp.int32)
    low = tile * 2 // 3
    own_sizes = lax.dynamic_slice_in_dim(block_sizes, owner * slots, slots, 0)
    total = jnp.sum(more_units(own_sizes, low, tile))
    ops = jnp.transpose(operator_blocks, (1, 2, 0))
    owner = owner[None]

    parts = [range(max(0, stop - 2), stop) for stop in range(slots, 1, -2)] + [range(0, 1)]
    bases, pool = pooled(owner, block_sizes, environment, parts, low)
    pool = pool_shifted(total, pool)
    here, one, two = [], [], []
    for i in range(len(parts)):
        here.append(shifted(tied(bases[i], here[i - 1] if i else pool), "region", OWN))
    pool_one = to_next(pool, "region")
    kept = pool.shape[0] // slots * (slots - 1)
    pool_two = to_second(pool[:kept], pool_one[:kept], "region")
    pools = [pool, pool_one, pool_two]
    for i in range(len(parts)):
        one.append(to_next(here[i], "region"))
        if i + 1 < len(parts):
            two.append(to_second(here[i], one[i], "region"))

    late = len(parts) - 2
    early = [(hop, i) for i in range(late) for hop in range(3)] + [(0, late)]
    rest = [(1, late), (2, late), (0, late + 1), (1, late + 1)]
    acc = None
    for chosen in (early, rest):
        blocks = [(here, one, two)[hop][i] for hop, i in chosen]
        wanted = [(hop, parts[i]) for hop, i in chosen]
        acc = stage(owner, join_in, block_sizes, wanted, blocks, pools, site_tensors, ops, acc, chosen is rest)
    return acc


def solution(mesh):
    placed = (
        P(("groups", "region"), None, None),
        P(("groups", "region"), None, None, None, None),
        P(),
        P("groups", None),
        P("groups"),
    )
    return jax.shard_map(
        per_device,
        mesh=mesh,
        in_specs=placed,
        out_specs=P(("groups", "region"), None, None),
        check_vma=False,
    )
```

profile of v0, /device:TPU:14, one launch (start us, length us, event | category | flops | bytes accessed | tf_op | source)
XLA Modules:
  0.0 173.6 jit_solution(1217228620930090752)
XLA Ops:
  0.0 1.4 fusion.1
  1.4 3.9 %shard_map.55 = (bf16[2,64,3264]{2,1,0:T(8,128)(2,1)}, bf16[2,64,3264]{2,1,0:T(8,128)(2,1)}, bf16[1,64,3264]{2,1,0:T(8,128)(2,1)}, bf16[10,16,3264]{2,1,0:T(8,128)(2,1)S(1)}) custom-call(s32[1]{0:T(128)} %bitcast.owner, s32[40]{0:T(128)} %sizes.5, bf16[5,96,3264]{2,1,0:T(8,128)(2,1)} %env_ref.1), custom_call_target="tpu_custom_call" | custom-call | flops 1000 | bytes 1024 | tf_op jit(solution)/shard_map/pallas_call | solution.py:81
  6.0 30.1 %conditional.1 = (bf16[10,16,3264]{2,1,0:T(8,128)(2,1)S(1)}) conditional(s32[]{:T(128)} %clamp.3, bf16[10,16,3264]{2,1,0:T(8,128)(2,1)S(1)} %get-tuple-element.37, bf16[10,16,3264]{2,1,0:T(8,128)(2,1)S(1)} %get-tuple-element.37, bf16[10,16,3264]{2,1,0:T(8,128)(2,1)S(1)} %get-tuple-element.37, ...), branch_computations={%region_1.2_spmd, %region_2.3_spmd, %region_3.4_spmd, %region_4.5_... | conditional | bytes 7557168 | solution.py:109
  6.1 2.7 %collective-permute-start.6 = (bf16[6,16,3264]{2,1,0:T(8,128)(2,1)S(1)}, bf16[6,16,3264]{2,1,0:T(8,128)(2,1)S(1)}, u32[]{:S(2)}, u32[]{:S(2)}) collective-permute-start(bf16[6,16,3264]{2,1,0:T(8,128)(2,1)S(1)} %slice.27), channel_id=1, source_target_pairs={{0,8},{1,9},{2,10},{3,11},{4,12},{5,13},{6,14},{7,15},{8,0},{9,1},... | collective-permute-start | bytes 1880072 | tf_op jit(solution)/shard_map/cond/branch_6_fun/ppermute | solution.py:19
  8.7 27.3 %collective-permute-done.6 = bf16[6,16,3264]{2,1,0:T(8,128)(2,1)S(1)} collective-permute-done((bf16[6,16,3264]{2,1,0:T(8,128)(2,1)S(1)}, bf16[6,16,3264]{2,1,0:T(8,128)(2,1)S(1)}, u32[]{:S(2)}, u32[]{:S(2)}) %collective-permute-start.6) | collective-permute-done | bytes 626720 | tf_op jit(solution)/shard_map/cond/branch_6_fun/ppermute | solution.py:19
  36.1 0.0 copy-start.2
  36.1 4.2 %collective-permute-start.17 = (bf16[10,16,3264]{2,1,0:T(8,128)(2,1)S(1)}, bf16[10,16,3264]{2,1,0:T(8,128)(2,1)S(1)}, u32[]{:S(2)}, u32[]{:S(2)}) collective-permute-start(bf16[10,16,3264]{2,1,0:T(8,128)(2,1)S(1)} %get-tuple-element.42.refs_4_), channel_id=1, source_target_pairs={{0,1},{1,2},{2,3},{3,4},{4,5},{5,6},{6,7},{8,9},{9,10},{10,11},{11... | collective-permute-start | bytes 3133448 | tf_op jit(solution)/shard_map/ppermute | solution.py:25
  40.3 3.1 %collective-permute-start.10 = (bf16[2,64,3264]{2,1,0:T(8,128)(2,1)}, bf16[2,64,3264]{2,1,0:T(8,128)(2,1)S(1)}, u32[]{:S(2)}, u32[]{:S(2)}) collective-permute-start(bf16[2,64,3264]{2,1,0:T(8,128)(2,1)} %get-tuple-element.38), channel_id=1, source_target_pairs={{0,8},{1,9},{2,10},{3,11},{4,12},{5,13},{6,14},{7,15},{8,0},{9,1},... | collective-permute-start | bytes 2506760 | tf_op jit(solution)/shard_map/ppermute | solution.py:19
  43.5 1.0 slice.35
  44.5 1.6 collective-permute-start.18
  46.1 0.1 copy.6
  46.2 0.1 copy.8.join
  46.3 33.0 %collective-permute-done.10.refs_0_ = bf16[2,64,3264]{2,1,0:T(8,128)(2,1)S(1)} collective-permute-done((bf16[2,64,3264]{2,1,0:T(8,128)(2,1)}, bf16[2,64,3264]{2,1,0:T(8,128)(2,1)S(1)}, u32[]{:S(2)}, u32[]{:S(2)}) %collective-permute-start.10) | collective-permute-done | bytes 835616 | tf_op jit(solution)/shard_map/ppermute | solution.py:19
  79.3 3.3 %collective-permute-start.11 = (bf16[2,64,3264]{2,1,0:T(8,128)(2,1)}, bf16[2,64,3264]{2,1,0:T(8,128)(2,1)S(1)}, u32[]{:S(2)}, u32[]{:S(2)}) collective-permute-start(bf16[2,64,3264]{2,1,0:T(8,128)(2,1)} %get-tuple-element.39), channel_id=1, source_target_pairs={{0,8},{1,9},{2,10},{3,11},{4,12},{5,13},{6,14},{7,15},{8,0},{9,1},... | collective-permute-start | bytes 2506760 | tf_op jit(solution)/shard_map/ppermute | solution.py:19
  82.6 1.9 %collective-permute-start.20 = (bf16[2,64,3264]{2,1,0:T(8,128)(2,1)S(1)}, bf16[2,64,3264]{2,1,0:T(8,128)(2,1)S(1)}, u32[]{:S(2)}, u32[]{:S(2)}) collective-permute-start(bf16[2,64,3264]{2,1,0:T(8,128)(2,1)S(1)} %collective-permute-done.10.refs_0_), channel_id=1, source_target_pairs={{0,1},{1,2},{2,3},{3,4},{4,5},{5,6},{6,7},{8,9},{9,10},{10,11},{11... | collective-permute-start | bytes 2506760 | tf_op jit(solution)/shard_map/ppermute | solution.py:25
  84.5 0.7 collective-permute-start.21
  85.3 0.1 slice_select_fusion
  85.4 1.9 %collective-permute-start.19 = (bf16[8,16,3264]{2,1,0:T(8,128)(2,1)S(1)}, bf16[8,16,3264]{2,1,0:T(8,128)(2,1)S(1)}, u32[]{:S(2)}, u32[]{:S(2)}) collective-permute-start(bf16[8,16,3264]{2,1,0:T(8,128)(2,1)S(1)} %slice_select_fusion), channel_id=1, source_target_pairs={{0,4},{1,2},{2,3},{4,5},{5,6},{6,7},{8,12},{9,10},{10,11},{12,13},... | collective-permute-start | bytes 2506760 | tf_op jit(solution)/shard_map/ppermute | solution.py:35
  87.3 30.9 %collective-permute-done.11.refs_3_ = bf16[2,64,3264]{2,1,0:T(8,128)(2,1)S(1)} collective-permute-done((bf16[2,64,3264]{2,1,0:T(8,128)(2,1)}, bf16[2,64,3264]{2,1,0:T(8,128)(2,1)S(1)}, u32[]{:S(2)}, u32[]{:S(2)}) %collective-permute-start.11) | collective-permute-done | bytes 835616 | tf_op jit(solution)/shard_map/ppermute | solution.py:19
  118.2 3.3 %collective-permute-start.15 = (bf16[1,64,3264]{2,1,0:T(8,128)(2,1)S(1)}, bf16[1,64,3264]{2,1,0:T(8,128)(2,1)S(1)}, u32[]{:S(2)}, u32[]{:S(2)}) collective-permute-start(bf16[1,64,3264]{2,1,0:T(8,128)(2,1)S(1)} %copy-done.4), channel_id=1, source_target_pairs={{0,8},{1,9},{2,10},{3,11},{4,12},{5,13},{6,14},{7,15},{8,0},{9,1},... | collective-permute-start | bytes 1253384 | tf_op jit(solution)/shard_map/ppermute | solution.py:19
  121.4 1.9 %collective-permute-start.12 = (bf16[2,64,3264]{2,1,0:T(8,128)(2,1)S(1)}, bf16[2,64,3264]{2,1,0:T(8,128)(2,1)S(1)}, u32[]{:S(2)}, u32[]{:S(2)}) collective-permute-start(bf16[2,64,3264]{2,1,0:T(8,128)(2,1)S(1)} %collective-permute-done.11.refs_3_), channel_id=1, source_target_pairs={{0,1},{1,2},{2,3},{3,4},{4,5},{5,6},{6,7},{8,9},{9,10},{10,11},{11... | collective-permute-start | bytes 2506760 | tf_op jit(solution)/shard_map/ppermute | solution.py:25
  123.4 0.7 collective-permute-start.13
  124.1 0.1 broadcast_select_fusion
  124.2 2.1 %collective-permute-start.22 = (bf16[2,64,3264]{2,1,0:T(8,128)(2,1)S(1)}, bf16[2,64,3264]{2,1,0:T(8,128)(2,1)S(1)}, u32[]{:S(2)}, u32[]{:S(2)}) collective-permute-start(bf16[2,64,3264]{2,1,0:T(8,128)(2,1)S(1)} %broadcast_select_fusion), channel_id=1, source_target_pairs={{0,4},{1,2},{2,3},{4,5},{5,6},{6,7},{8,12},{9,10},{10,11},{12,13},... | collective-permute-start | bytes 2506760 | tf_op jit(solution)/shard_map/ppermute | solution.py:35
  126.3 12.8 %collective-permute-done.15.refs_2_ = bf16[1,64,3264]{2,1,0:T(8,128)(2,1)S(1)} collective-permute-done((bf16[1,64,3264]{2,1,0:T(8,128)(2,1)S(1)}, bf16[1,64,3264]{2,1,0:T(8,128)(2,1)S(1)}, u32[]{:S(2)}, u32[]{:S(2)}) %collective-permute-start.15) | collective-permute-done | bytes 417824 | tf_op jit(solution)/shard_map/ppermute | solution.py:19
  139.0 1.9 %collective-permute-start.16 = (bf16[1,64,3264]{2,1,0:T(8,128)(2,1)S(1)}, bf16[1,64,3264]{2,1,0:T(8,128)(2,1)S(1)}, u32[]{:S(2)}, u32[]{:S(2)}) collective-permute-start(bf16[1,64,3264]{2,1,0:T(8,128)(2,1)S(1)} %collective-permute-done.15.refs_2_), channel_id=1, source_target_pairs={{0,1},{1,2},{2,3},{3,4},{4,5},{5,6},{6,7},{8,9},{9,10},{10,11},{11... | collective-permute-start | bytes 1253384 | tf_op jit(solution)/shard_map/ppermute | solution.py:25
  141.0 0.1 broadcast_select_fusion.1
  141.1 1.9 %collective-permute-start.14 = (bf16[2,64,3264]{2,1,0:T(8,128)(2,1)S(1)}, bf16[2,64,3264]{2,1,0:T(8,128)(2,1)S(1)}, u32[]{:S(2)}, u32[]{:S(2)}) collective-permute-start(bf16[2,64,3264]{2,1,0:T(8,128)(2,1)S(1)} %broadcast_select_fusion.1), channel_id=1, source_target_pairs={{0,4},{1,2},{2,3},{4,5},{5,6},{6,7},{8,12},{9,10},{10,11},{12,13},... | collective-permute-start | bytes 2506760 | tf_op jit(solution)/shard_map/ppermute | solution.py:35
  143.1 1.5 collective-permute-done.22.refs_2_
  144.6 12.4 %shard_map.56.refs_9_ = f32[5,3264,128]{2,1,0:T(8,128)S(1)} custom-call(s32[1]{0:T(128)} %bitcast.owner, s32[40,4]{1,0:T(8,128)S(1)} %copy.8.join, s32[40]{0:T(128)S(1)} %copy-done, bf16[2,64,3264]{2,1,0:T(8,128)(2,1)S(1)} %collective-permute-done.10.refs_0_, bf16[2,64,3264]{2,1,0:T(8,128)(2,1)S(1)} %collective-permute-done.20.refs_1_, ...), custom_call_target="tpu_custom_call" | custom-call | flops 10000000000 | bytes 1048576 | tf_op jit(solution)/shard_map/pallas_call | solution.py:241
  157.0 1.3 collective-permute-done.14.refs_1_
  158.2 15.4 %shard_map.57 = bf16[5,96,3264]{2,1,0:T(8,128)(2,1)} custom-call(s32[1]{0:T(128)} %bitcast.owner, s32[40,4]{1,0:T(8,128)S(1)} %copy.8.join, s32[40]{0:T(128)S(1)} %copy-done, bf16[2,64,3264]{2,1,0:T(8,128)(2,1)S(1)} %collective-permute-done.12.refs_0_, bf16[2,64,3264]{2,1,0:T(8,128)(2,1)S(1)} %collective-permute-done.14.refs_1_, ...), custom_call_target="tpu_custom_call" | custom-call | flops 10000000000 | bytes 1048576 | tf_op jit(solution)/shard_map/pallas_call | solution.py:241
  (19 shorter events, 0.1 us)
Async XLA Ops:
  6.1 30.0 %collective-permute-start.6 = (bf16[6,16,3264]{2,1,0:T(8,128)(2,1)S(1)}, bf16[6,16,3264]{2,1,0:T(8,128)(2,1)S(1)}, u32[]{:S(2)}, u32[]{:S(2)}) collective-permute-start(bf16[6,16,3264]{2,1,0:T(8,128)(2,1)S(1)} %slice.27), channel_id=1, source_target_pairs={{0,8},{1,9},{2,10},{3,11},{4,12},{5,13},{6,14},{7,15},{8,0},{9,1},... | collective-permute-start | bytes 1880072 | tf_op jit(solution)/shard_map/cond/branch_6_fun/ppermute | solution.py:19
  36.1 10.0 %copy-start.2 = (bf16[34,4,34]{2,1,0:T(4,128)(2,1)S(1)}, bf16[34,4,34]{2,1,0:T(4,128)(2,1)}, u32[]{:S(2)}) copy-start(bf16[34,4,34]{2,1,0:T(4,128)(2,1)} %param.18) | copy-start | bytes 27748
  36.1 10.1 %copy-start.3 = (s32[40,4]{0,1:T(4,128)S(1)}, s32[40,4]{0,1:T(4,128)}, u32[]{:S(2)}) copy-start(s32[40,4]{0,1:T(4,128)} %param.19) | copy-start | bytes 1924
  36.1 49.1 %collective-permute-start.17 = (bf16[10,16,3264]{2,1,0:T(8,128)(2,1)S(1)}, bf16[10,16,3264]{2,1,0:T(8,128)(2,1)S(1)}, u32[]{:S(2)}, u32[]{:S(2)}) collective-permute-start(bf16[10,16,3264]{2,1,0:T(8,128)(2,1)S(1)} %get-tuple-element.42.refs_4_), channel_id=1, source_target_pairs={{0,1},{1,2},{2,3},{3,4},{4,5},{5,6},{6,7},{8,9},{9,10},{10,11},{11... | collective-permute-start | bytes 3133448 | tf_op jit(solution)/shard_map/ppermute | solution.py:25
  40.3 39.0 %collective-permute-start.10 = (bf16[2,64,3264]{2,1,0:T(8,128)(2,1)}, bf16[2,64,3264]{2,1,0:T(8,128)(2,1)S(1)}, u32[]{:S(2)}, u32[]{:S(2)}) collective-permute-start(bf16[2,64,3264]{2,1,0:T(8,128)(2,1)} %get-tuple-element.38), channel_id=1, source_target_pairs={{0,8},{1,9},{2,10},{3,11},{4,12},{5,13},{6,14},{7,15},{8,0},{9,1},... | collective-permute-start | bytes 2506760 | tf_op jit(solution)/shard_map/ppermute | solution.py:19
  44.5 40.7 %collective-permute-start.18 = (bf16[8,16,3264]{2,1,0:T(8,128)(2,1)}, bf16[8,16,3264]{2,1,0:T(8,128)(2,1)}, u32[]{:S(2)}, u32[]{:S(2)}) collective-permute-start(bf16[8,16,3264]{2,1,0:T(8,128)(2,1)} %slice.35), channel_id=1, source_target_pairs={{2,0},{10,8},{18,16},{26,24}} | collective-permute-start | bytes 2506760 | tf_op jit(solution)/shard_map/ppermute | solution.py:32
  79.3 38.8 %copy-start.4 = (bf16[1,64,3264]{2,1,0:T(8,128)(2,1)S(1)}, bf16[1,64,3264]{2,1,0:T(8,128)(2,1)}, u32[]{:S(2)}) copy-start(bf16[1,64,3264]{2,1,0:T(8,128)(2,1)} %get-tuple-element.41) | copy-start | bytes 1253380
  79.3 38.8 %collective-permute-start.11 = (bf16[2,64,3264]{2,1,0:T(8,128)(2,1)}, bf16[2,64,3264]{2,1,0:T(8,128)(2,1)S(1)}, u32[]{:S(2)}, u32[]{:S(2)}) collective-permute-start(bf16[2,64,3264]{2,1,0:T(8,128)(2,1)} %get-tuple-element.39), channel_id=1, source_target_pairs={{0,8},{1,9},{2,10},{3,11},{4,12},{5,13},{6,14},{7,15},{8,0},{9,1},... | collective-permute-start | bytes 2506760 | tf_op jit(solution)/shard_map/ppermute | solution.py:19
  82.6 40.7 %collective-permute-start.20 = (bf16[2,64,3264]{2,1,0:T(8,128)(2,1)S(1)}, bf16[2,64,3264]{2,1,0:T(8,128)(2,1)S(1)}, u32[]{:S(2)}, u32[]{:S(2)}) collective-permute-start(bf16[2,64,3264]{2,1,0:T(8,128)(2,1)S(1)} %collective-permute-done.10.refs_0_), channel_id=1, source_target_pairs={{0,1},{1,2},{2,3},{3,4},{4,5},{5,6},{6,7},{8,9},{9,10},{10,11},{11... | collective-permute-start | bytes 2506760 | tf_op jit(solution)/shard_map/ppermute | solution.py:25
  84.5 39.6 %collective-permute-start.21 = (bf16[2,64,3264]{2,1,0:T(8,128)(2,1)S(1)}, bf16[2,64,3264]{2,1,0:T(8,128)(2,1)S(1)}, u32[]{:S(2)}, u32[]{:S(2)}) collective-permute-start(bf16[2,64,3264]{2,1,0:T(8,128)(2,1)S(1)} %collective-permute-done.10.refs_0_), channel_id=1, source_target_pairs={{2,0},{10,8},{18,16},{26,24}} | collective-permute-start | bytes 2506760 | tf_op jit(solution)/shard_map/ppermute | solution.py:32
  85.4 57.7 %collective-permute-start.19 = (bf16[8,16,3264]{2,1,0:T(8,128)(2,1)S(1)}, bf16[8,16,3264]{2,1,0:T(8,128)(2,1)S(1)}, u32[]{:S(2)}, u32[]{:S(2)}) collective-permute-start(bf16[8,16,3264]{2,1,0:T(8,128)(2,1)S(1)} %slice_select_fusion), channel_id=1, source_target_pairs={{0,4},{1,2},{2,3},{4,5},{5,6},{6,7},{8,12},{9,10},{10,11},{12,13},... | collective-permute-start | bytes 2506760 | tf_op jit(solution)/shard_map/ppermute | solution.py:35
  118.2 20.9 %collective-permute-start.15 = (bf16[1,64,3264]{2,1,0:T(8,128)(2,1)S(1)}, bf16[1,64,3264]{2,1,0:T(8,128)(2,1)S(1)}, u32[]{:S(2)}, u32[]{:S(2)}) collective-permute-start(bf16[1,64,3264]{2,1,0:T(8,128)(2,1)S(1)} %copy-done.4), channel_id=1, source_target_pairs={{0,8},{1,9},{2,10},{3,11},{4,12},{5,13},{6,14},{7,15},{8,0},{9,1},... | collective-permute-start | bytes 1253384 | tf_op jit(solution)/shard_map/ppermute | solution.py:19
  121.4 19.5 %collective-permute-start.12 = (bf16[2,64,3264]{2,1,0:T(8,128)(2,1)S(1)}, bf16[2,64,3264]{2,1,0:T(8,128)(2,1)S(1)}, u32[]{:S(2)}, u32[]{:S(2)}) collective-permute-start(bf16[2,64,3264]{2,1,0:T(8,128)(2,1)S(1)} %collective-permute-done.11.refs_3_), channel_id=1, source_target_pairs={{0,1},{1,2},{2,3},{3,4},{4,5},{5,6},{6,7},{8,9},{9,10},{10,11},{11... | collective-permute-start | bytes 2506760 | tf_op jit(solution)/shard_map/ppermute | solution.py:25
  123.4 17.6 %collective-permute-start.13 = (bf16[2,64,3264]{2,1,0:T(8,128)(2,1)S(1)}, bf16[2,64,3264]{2,1,0:T(8,128)(2,1)S(1)}, u32[]{:S(2)}, u32[]{:S(2)}) collective-permute-start(bf16[2,64,3264]{2,1,0:T(8,128)(2,1)S(1)} %collective-permute-done.11.refs_3_), channel_id=1, source_target_pairs={{2,0},{10,8},{18,16},{26,24}} | collective-permute-start | bytes 2506760 | tf_op jit(solution)/shard_map/ppermute | solution.py:32
  124.2 20.4 %copy-start = (s32[40]{0:T(128)S(1)}, s32[40]{0:T(128)}, u32[]{:S(2)}) copy-start(s32[40]{0:T(128)} %sizes.5) | copy-start | bytes 484
  124.2 20.3 %copy-start.1 = (bf16[5,1,4,96,96]{4,3,2,1,0:T(8,128)(2,1)S(1)}, bf16[5,1,4,96,96]{4,3,2,1,0:T(8,128)(2,1)}, u32[]{:S(2)}) copy-start(bf16[5,1,4,96,96]{4,3,2,1,0:T(8,128)(2,1)} %refs_7_.3) | copy-start | bytes 1105924
  124.2 20.3 %collective-permute-start.22 = (bf16[2,64,3264]{2,1,0:T(8,128)(2,1)S(1)}, bf16[2,64,3264]{2,1,0:T(8,128)(2,1)S(1)}, u32[]{:S(2)}, u32[]{:S(2)}) collective-permute-start(bf16[2,64,3264]{2,1,0:T(8,128)(2,1)S(1)} %broadcast_select_fusion), channel_id=1, source_target_pairs={{0,4},{1,2},{2,3},{4,5},{5,6},{6,7},{8,12},{9,10},{10,11},{12,13},... | collective-permute-start | bytes 2506760 | tf_op jit(solution)/shard_map/ppermute | solution.py:35
  139.0 17.9 %collective-permute-start.16 = (bf16[1,64,3264]{2,1,0:T(8,128)(2,1)S(1)}, bf16[1,64,3264]{2,1,0:T(8,128)(2,1)S(1)}, u32[]{:S(2)}, u32[]{:S(2)}) collective-permute-start(bf16[1,64,3264]{2,1,0:T(8,128)(2,1)S(1)} %collective-permute-done.15.refs_2_), channel_id=1, source_target_pairs={{0,1},{1,2},{2,3},{3,4},{4,5},{5,6},{6,7},{8,9},{9,10},{10,11},{11... | collective-permute-start | bytes 1253384 | tf_op jit(solution)/shard_map/ppermute | solution.py:25
  141.1 17.1 %collective-permute-start.14 = (bf16[2,64,3264]{2,1,0:T(8,128)(2,1)S(1)}, bf16[2,64,3264]{2,1,0:T(8,128)(2,1)S(1)}, u32[]{:S(2)}, u32[]{:S(2)}) collective-permute-start(bf16[2,64,3264]{2,1,0:T(8,128)(2,1)S(1)} %broadcast_select_fusion.1), channel_id=1, source_target_pairs={{0,4},{1,2},{2,3},{4,5},{5,6},{6,7},{8,12},{9,10},{10,11},{12,13},... | collective-permute-start | bytes 2506760 | tf_op jit(solution)/shard_map/ppermute | solution.py:35
where the time goes:
time: 176 us; the launch traced here: 174 us
  waiting for transfers between devices  107 us (61%)
  Pallas kernels  31.7 us (18%)
  starting transfers between devices  31.2 us (18%)
    ppermute x4, waiting for transfers between devices, shifted(): lax.ppermute(value, axis, [(source, (source + steps) % count) for source...  104 us
    pallas_call x2, Pallas kernels, stage(): pl.pallas_call(functools.partial(stage_kernel, first, last, tuple(wanted)...  27.8 us
    ppermute x4, starting transfers between devices, shifted(): lax.ppermute(value, axis, [(source, (source + steps) % count) for source...  12.4 us
    ppermute x4, starting transfers between devices, to_next(): return lax.ppermute(value, axis, pairs)  9.96 us
    ppermute x3, starting transfers between devices, to_second(): lax.ppermute(sent, axis, [(r + a, r + b) for r in regions for a, b in ste...  5.89 us
    pallas_call x1, Pallas kernels, pooled(): pl.pallas_call(functools.partial(pool_kernel, slots, parts, low, tile), o...  3.92 us
  transfers between devices with their start and end apart: 14, of which 6 were waited for; matrix products, arithmetic and copies ran while one was open for 1% of the time, Pallas kernels for 7%

commit v1 on v0

--- a/solution.py
+++ b/solution.py
@@ -170,13 +170,18 @@
             both = lax.dot_general(spread_rows, pick, (((1,), (1,)), ((), ())), preferred_element_type=jnp.float32)
             mix[q] = jnp.where(same, both, 0.0).astype(jnp.bfloat16)
 
-    acc[...] = jnp.zeros(acc.shape, jnp.float32) if first else acc_in[b]
     own_size = sizes[base + b]
     for q in range(states):
         a = join[base + b, q]
         place = jnp.int32(-1)
         for at, (hop, slot, _, _) in enumerate(listed):
             place = jnp.where(a - base == slot - hop * slots, at, place)
+
+        if q == 0:
+
+            @pl.when((a < 0) | (place < 0))
+            def _():
+                acc[...] = jnp.zeros(acc.shape, jnp.float32) if first else acc_in[b]
 
         @pl.when((a >= 0) & (place >= 0))
         def _():
@@ -199,7 +204,12 @@
                 vb[g * span : (g + 2) * span, :] = v
             for g in range(0, tile * chans, CHUNK):
                 some = slice(g, g + CHUNK)
-                acc[some, :] += jnp.dot(vb[some, :], gy, preferred_element_type=jnp.float32)
+                total = jnp.dot(vb[some, :], gy, preferred_element_type=jnp.float32)
+                if q:
+                    total += acc[some, :]
+                elif not first:
+                    total += acc_in[b, some, :]
+                acc[some, :] = total
 
     if last:
         for w in range(chans):

time: 176 us -> 173 us (0.983)
  the two profiles are of different devices: /device:TPU:14 before, /device:TPU:24 now
where the time goes in v1:
time: 173 us; the launch traced here: 170 us
  waiting for transfers between devices  117 us (68%)
  Pallas kernels  30.5 us (18%)
  starting transfers between devices  18 us (10%)
  other arithmetic  1.73 us (1%)
    ppermute x4, waiting for transfers between devices, shifted(): lax.ppermute(value, axis, [(source, (source + steps) % count) for source...  116 us
    pallas_call x2, Pallas kernels, stage(): pl.pallas_call(functools.partial(stage_kernel, first, last, tuple(wanted)...  26.6 us
    ppermute x4, starting transfers between devices, to_next(): return lax.ppermute(value, axis, pairs)  8.66 us
    ppermute x3, starting transfers between devices, to_second(): lax.ppermute(sent, axis, [(r + a, r + b) for r in regions for a, b in ste...  5.89 us
    pallas_call x1, Pallas kernels, pooled(): pl.pallas_call(functools.partial(pool_kernel, slots, parts, low, tile), o...  3.92 us
  transfers between devices with their start and end apart: 14, of which 6 were waited for; matrix products, arithmetic and copies ran while one was open for 1% of the time, Pallas kernels for 8%

profile of v1, /device:TPU:24, one launch (start us, length us, event | category | flops | bytes accessed | tf_op | source)
XLA Modules:
  0.0 169.9 jit_solution(15930926773593047977)
XLA Ops:
  0.0 1.4 fusion.1
  1.4 3.9 %shard_map.55 = (bf16[2,64,3264]{2,1,0:T(8,128)(2,1)}, bf16[2,64,3264]{2,1,0:T(8,128)(2,1)}, bf16[1,64,3264]{2,1,0:T(8,128)(2,1)}, bf16[10,16,3264]{2,1,0:T(8,128)(2,1)S(1)}) custom-call(s32[1]{0:T(128)} %bitcast.owner, s32[40]{0:T(128)} %sizes.5, bf16[5,96,3264]{2,1,0:T(8,128)(2,1)} %env_ref.1), custom_call_target="tpu_custom_call" | custom-call | flops 1000 | bytes 1024 | tf_op jit(solution)/shard_map/pallas_call | solution.py:81
  6.0 30.9 %conditional.1 = (bf16[10,16,3264]{2,1,0:T(8,128)(2,1)S(1)}) conditional(s32[]{:T(128)} %clamp.3, bf16[10,16,3264]{2,1,0:T(8,128)(2,1)S(1)} %get-tuple-element.37, bf16[10,16,3264]{2,1,0:T(8,128)(2,1)S(1)} %get-tuple-element.37, bf16[10,16,3264]{2,1,0:T(8,128)(2,1)S(1)} %get-tuple-element.37, ...), branch_computations={%region_1.2_spmd, %region_2.3_spmd, %region_3.4_spmd, %region_4.5_... | conditional | bytes 7557168 | solution.py:109
  6.0 0.1 slice.28
  6.1 0.4 collective-permute-start.7
  6.5 30.3 %collective-permute-done.7 = bf16[7,16,3264]{2,1,0:T(8,128)(2,1)S(1)} collective-permute-done((bf16[7,16,3264]{2,1,0:T(8,128)(2,1)S(1)}, bf16[7,16,3264]{2,1,0:T(8,128)(2,1)S(1)}, u32[]{:S(2)}, u32[]{:S(2)}) %collective-permute-start.7) | collective-permute-done | bytes 731168 | tf_op jit(solution)/shard_map/cond/branch_7_fun/ppermute | solution.py:19
  36.9 0.0 copy-start.3
  36.9 2.8 %collective-permute-start.17 = (bf16[10,16,3264]{2,1,0:T(8,128)(2,1)S(1)}, bf16[10,16,3264]{2,1,0:T(8,128)(2,1)S(1)}, u32[]{:S(2)}, u32[]{:S(2)}) collective-permute-start(bf16[10,16,3264]{2,1,0:T(8,128)(2,1)S(1)} %get-tuple-element.42.refs_4_), channel_id=1, source_target_pairs={{0,1},{1,2},{2,3},{3,4},{4,5},{5,6},{6,7},{8,9},{9,10},{10,11},{11... | collective-permute-start | bytes 3133448 | tf_op jit(solution)/shard_map/ppermute | solution.py:25
  39.7 0.1 collective-permute-start.10
  39.7 1.0 slice.35
  40.7 1.6 collective-permute-start.18
  42.3 0.1 copy.6
  42.4 0.1 copy.8.join
  42.5 34.5 %collective-permute-done.10.refs_0_ = bf16[2,64,3264]{2,1,0:T(8,128)(2,1)S(1)} collective-permute-done((bf16[2,64,3264]{2,1,0:T(8,128)(2,1)}, bf16[2,64,3264]{2,1,0:T(8,128)(2,1)S(1)}, u32[]{:S(2)}, u32[]{:S(2)}) %collective-permute-start.10) | collective-permute-done | bytes 835616 | tf_op jit(solution)/shard_map/ppermute | solution.py:19
  77.1 2.1 %collective-permute-start.20 = (bf16[2,64,3264]{2,1,0:T(8,128)(2,1)S(1)}, bf16[2,64,3264]{2,1,0:T(8,128)(2,1)S(1)}, u32[]{:S(2)}, u32[]{:S(2)}) collective-permute-start(bf16[2,64,3264]{2,1,0:T(8,128)(2,1)S(1)} %collective-permute-done.10.refs_0_), channel_id=1, source_target_pairs={{0,1},{1,2},{2,3},{3,4},{4,5},{5,6},{6,7},{8,9},{9,10},{10,11},{11... | collective-permute-start | bytes 2506760 | tf_op jit(solution)/shard_map/ppermute | solution.py:25
  79.1 0.7 collective-permute-start.21
  79.9 0.1 slice_select_fusion
  80.0 1.9 %collective-permute-start.19 = (bf16[8,16,3264]{2,1,0:T(8,128)(2,1)S(1)}, bf16[8,16,3264]{2,1,0:T(8,128)(2,1)S(1)}, u32[]{:S(2)}, u32[]{:S(2)}) collective-permute-start(bf16[8,16,3264]{2,1,0:T(8,128)(2,1)S(1)} %slice_select_fusion), channel_id=1, source_target_pairs={{0,4},{1,2},{2,3},{4,5},{5,6},{6,7},{8,12},{9,10},{10,11},{12,13},... | collective-permute-start | bytes 2506760 | tf_op jit(solution)/shard_map/ppermute | solution.py:35
  81.9 34.3 %collective-permute-done.11.refs_3_ = bf16[2,64,3264]{2,1,0:T(8,128)(2,1)S(1)} collective-permute-done((bf16[2,64,3264]{2,1,0:T(8,128)(2,1)}, bf16[2,64,3264]{2,1,0:T(8,128)(2,1)S(1)}, u32[]{:S(2)}, u32[]{:S(2)}) %collective-permute-start.11) | collective-permute-done | bytes 835616 | tf_op jit(solution)/shard_map/ppermute | solution.py:19
  116.3 1.9 %collective-permute-start.12 = (bf16[2,64,3264]{2,1,0:T(8,128)(2,1)S(1)}, bf16[2,64,3264]{2,1,0:T(8,128)(2,1)S(1)}, u32[]{:S(2)}, u32[]{:S(2)}) collective-permute-start(bf16[2,64,3264]{2,1,0:T(8,128)(2,1)S(1)} %collective-permute-done.11.refs_3_), channel_id=1, source_target_pairs={{0,1},{1,2},{2,3},{3,4},{4,5},{5,6},{6,7},{8,9},{9,10},{10,11},{11... | collective-permute-start | bytes 2506760 | tf_op jit(solution)/shard_map/ppermute | solution.py:25
  118.2 0.7 collective-permute-start.13
  118.9 0.1 broadcast_select_fusion
  119.1 0.0 copy-start.1
  119.1 2.1 %collective-permute-start.22 = (bf16[2,64,3264]{2,1,0:T(8,128)(2,1)S(1)}, bf16[2,64,3264]{2,1,0:T(8,128)(2,1)S(1)}, u32[]{:S(2)}, u32[]{:S(2)}) collective-permute-start(bf16[2,64,3264]{2,1,0:T(8,128)(2,1)S(1)} %broadcast_select_fusion), channel_id=1, source_target_pairs={{0,4},{1,2},{2,3},{4,5},{5,6},{6,7},{8,12},{9,10},{10,11},{12,13},... | collective-permute-start | bytes 2506760 | tf_op jit(solution)/shard_map/ppermute | solution.py:35
  121.1 16.6 %collective-permute-done.15.refs_2_ = bf16[1,64,3264]{2,1,0:T(8,128)(2,1)S(1)} collective-permute-done((bf16[1,64,3264]{2,1,0:T(8,128)(2,1)S(1)}, bf16[1,64,3264]{2,1,0:T(8,128)(2,1)S(1)}, u32[]{:S(2)}, u32[]{:S(2)}) %collective-permute-start.15) | collective-permute-done | bytes 417824 | tf_op jit(solution)/shard_map/ppermute | solution.py:19
  137.7 1.9 %collective-permute-start.16 = (bf16[1,64,3264]{2,1,0:T(8,128)(2,1)S(1)}, bf16[1,64,3264]{2,1,0:T(8,128)(2,1)S(1)}, u32[]{:S(2)}, u32[]{:S(2)}) collective-permute-start(bf16[1,64,3264]{2,1,0:T(8,128)(2,1)S(1)} %collective-permute-done.15.refs_2_), channel_id=1, source_target_pairs={{0,1},{1,2},{2,3},{3,4},{4,5},{5,6},{6,7},{8,9},{9,10},{10,11},{11... | collective-permute-start | bytes 1253384 | tf_op jit(solution)/shard_map/ppermute | solution.py:25
  139.6 0.5 collective-permute-done.12.refs_0_
  140.2 0.1 broadcast_select_fusion.1
  140.3 1.9 %collective-permute-start.14 = (bf16[2,64,3264]{2,1,0:T(8,128)(2,1)S(1)}, bf16[2,64,3264]{2,1,0:T(8,128)(2,1)S(1)}, u32[]{:S(2)}, u32[]{:S(2)}) collective-permute-start(bf16[2,64,3264]{2,1,0:T(8,128)(2,1)S(1)} %broadcast_select_fusion.1), channel_id=1, source_target_pairs={{0,4},{1,2},{2,3},{4,5},{5,6},{6,7},{8,12},{9,10},{10,11},{12,13},... | collective-permute-start | bytes 2506760 | tf_op jit(solution)/shard_map/ppermute | solution.py:35
  142.2 1.1 collective-permute-done.22.refs_2_
  143.3 14.1 %shard_map.56.refs_9_ = f32[5,3264,128]{2,1,0:T(8,128)S(1)} custom-call(s32[1]{0:T(128)} %bitcast.owner, s32[40,4]{1,0:T(8,128)S(1)} %copy.8.join, s32[40]{0:T(128)S(1)} %copy-done, bf16[2,64,3264]{2,1,0:T(8,128)(2,1)S(1)} %collective-permute-done.10.refs_0_, bf16[2,64,3264]{2,1,0:T(8,128)(2,1)S(1)} %collective-permute-done.20.refs_1_, ...), custom_call_target="tpu_custom_call" | custom-call | flops 10000000000 | bytes 1048576 | tf_op jit(solution)/shard_map/pallas_call | solution.py:251
  157.4 12.5 %shard_map.57 = bf16[5,96,3264]{2,1,0:T(8,128)(2,1)} custom-call(s32[1]{0:T(128)} %bitcast.owner, s32[40,4]{1,0:T(8,128)S(1)} %copy.8.join, s32[40]{0:T(128)S(1)} %copy-done, bf16[2,64,3264]{2,1,0:T(8,128)(2,1)S(1)} %collective-permute-done.12.refs_0_, bf16[2,64,3264]{2,1,0:T(8,128)(2,1)S(1)} %collective-permute-done.14.refs_1_, ...), custom_call_target="tpu_custom_call" | custom-call | flops 10000000000 | bytes 1048576 | tf_op jit(solution)/shard_map/pallas_call | solution.py:251
  (19 shorter events, 0.1 us)
Async XLA Ops:
  6.1 30.7 %collective-permute-start.7 = (bf16[7,16,3264]{2,1,0:T(8,128)(2,1)S(1)}, bf16[7,16,3264]{2,1,0:T(8,128)(2,1)S(1)}, u32[]{:S(2)}, u32[]{:S(2)}) collective-permute-start(bf16[7,16,3264]{2,1,0:T(8,128)(2,1)S(1)} %slice.28), channel_id=1, source_target_pairs={{0,8},{1,9},{2,10},{3,11},{4,12},{5,13},{6,14},{7,15},{8,0},{9,1},... | collective-permute-start | bytes 2193416 | tf_op jit(solution)/shard_map/cond/branch_7_fun/ppermute | solution.py:19
  36.9 5.4 %copy-start.2 = (bf16[34,4,34]{2,1,0:T(4,128)(2,1)S(1)}, bf16[34,4,34]{2,1,0:T(4,128)(2,1)}, u32[]{:S(2)}) copy-start(bf16[34,4,34]{2,1,0:T(4,128)(2,1)} %param.18) | copy-start | bytes 27748
  36.9 5.6 %copy-start.3 = (s32[40,4]{0,1:T(4,128)S(1)}, s32[40,4]{0,1:T(4,128)}, u32[]{:S(2)}) copy-start(s32[40,4]{0,1:T(4,128)} %param.19) | copy-start | bytes 1924
  36.9 43.0 %collective-permute-start.17 = (bf16[10,16,3264]{2,1,0:T(8,128)(2,1)S(1)}, bf16[10,16,3264]{2,1,0:T(8,128)(2,1)S(1)}, u32[]{:S(2)}, u32[]{:S(2)}) collective-permute-start(bf16[10,16,3264]{2,1,0:T(8,128)(2,1)S(1)} %get-tuple-element.42.refs_4_), channel_id=1, source_target_pairs={{0,1},{1,2},{2,3},{3,4},{4,5},{5,6},{6,7},{8,9},{9,10},{10,11},{11... | collective-permute-start | bytes 3133448 | tf_op jit(solution)/shard_map/ppermute | solution.py:25
  39.7 37.4 %collective-permute-start.10 = (bf16[2,64,3264]{2,1,0:T(8,128)(2,1)}, bf16[2,64,3264]{2,1,0:T(8,128)(2,1)S(1)}, u32[]{:S(2)}, u32[]{:S(2)}) collective-permute-start(bf16[2,64,3264]{2,1,0:T(8,128)(2,1)} %get-tuple-element.38), channel_id=1, source_target_pairs={{0,8},{1,9},{2,10},{3,11},{4,12},{5,13},{6,14},{7,15},{8,0},{9,1},... | collective-permute-start | bytes 2506760 | tf_op jit(solution)/shard_map/ppermute | solution.py:19
  40.7 39.1 %collective-permute-start.18 = (bf16[8,16,3264]{2,1,0:T(8,128)(2,1)}, bf16[8,16,3264]{2,1,0:T(8,128)(2,1)}, u32[]{:S(2)}, u32[]{:S(2)}) collective-permute-start(bf16[8,16,3264]{2,1,0:T(8,128)(2,1)} %slice.35), channel_id=1, source_target_pairs={{2,0},{10,8},{18,16},{26,24}} | collective-permute-start | bytes 2506760 | tf_op jit(solution)/shard_map/ppermute | solution.py:32
  77.1 39.2 %copy-start.4 = (bf16[1,64,3264]{2,1,0:T(8,128)(2,1)S(1)}, bf16[1,64,3264]{2,1,0:T(8,128)(2,1)}, u32[]{:S(2)}) copy-start(bf16[1,64,3264]{2,1,0:T(8,128)(2,1)} %get-tuple-element.41) | copy-start | bytes 1253380
  77.1 39.2 %collective-permute-start.11 = (bf16[2,64,3264]{2,1,0:T(8,128)(2,1)}, bf16[2,64,3264]{2,1,0:T(8,128)(2,1)S(1)}, u32[]{:S(2)}, u32[]{:S(2)}) collective-permute-start(bf16[2,64,3264]{2,1,0:T(8,128)(2,1)} %get-tuple-element.39), channel_id=1, source_target_pairs={{0,8},{1,9},{2,10},{3,11},{4,12},{5,13},{6,14},{7,15},{8,0},{9,1},... | collective-permute-start | bytes 2506760 | tf_op jit(solution)/shard_map/ppermute | solution.py:19
  77.1 41.1 %collective-permute-start.20 = (bf16[2,64,3264]{2,1,0:T(8,128)(2,1)S(1)}, bf16[2,64,3264]{2,1,0:T(8,128)(2,1)S(1)}, u32[]{:S(2)}, u32[]{:S(2)}) collective-permute-start(bf16[2,64,3264]{2,1,0:T(8,128)(2,1)S(1)} %collective-permute-done.10.refs_0_), channel_id=1, source_target_pairs={{0,1},{1,2},{2,3},{3,4},{4,5},{5,6},{6,7},{8,9},{9,10},{10,11},{11... | collective-permute-start | bytes 2506760 | tf_op jit(solution)/shard_map/ppermute | solution.py:25
  79.1 39.8 %collective-permute-start.21 = (bf16[2,64,3264]{2,1,0:T(8,128)(2,1)S(1)}, bf16[2,64,3264]{2,1,0:T(8,128)(2,1)S(1)}, u32[]{:S(2)}, u32[]{:S(2)}) collective-permute-start(bf16[2,64,3264]{2,1,0:T(8,128)(2,1)S(1)} %collective-permute-done.10.refs_0_), channel_id=1, source_target_pairs={{2,0},{10,8},{18,16},{26,24}} | collective-permute-start | bytes 2506760 | tf_op jit(solution)/shard_map/ppermute | solution.py:32
  80.0 62.3 %collective-permute-start.19 = (bf16[8,16,3264]{2,1,0:T(8,128)(2,1)S(1)}, bf16[8,16,3264]{2,1,0:T(8,128)(2,1)S(1)}, u32[]{:S(2)}, u32[]{:S(2)}) collective-permute-start(bf16[8,16,3264]{2,1,0:T(8,128)(2,1)S(1)} %slice_select_fusion), channel_id=1, source_target_pairs={{0,4},{1,2},{2,3},{4,5},{5,6},{6,7},{8,12},{9,10},{10,11},{12,13},... | collective-permute-start | bytes 2506760 | tf_op jit(solution)/shard_map/ppermute | solution.py:35
  116.3 21.5 %collective-permute-start.15 = (bf16[1,64,3264]{2,1,0:T(8,128)(2,1)S(1)}, bf16[1,64,3264]{2,1,0:T(8,128)(2,1)S(1)}, u32[]{:S(2)}, u32[]{:S(2)}) collective-permute-start(bf16[1,64,3264]{2,1,0:T(8,128)(2,1)S(1)} %copy-done.4), channel_id=1, source_target_pairs={{0,8},{1,9},{2,10},{3,11},{4,12},{5,13},{6,14},{7,15},{8,0},{9,1},... | collective-permute-start | bytes 1253384 | tf_op jit(solution)/shard_map/ppermute | solution.py:19
  116.3 23.9 %collective-permute-start.12 = (bf16[2,64,3264]{2,1,0:T(8,128)(2,1)S(1)}, bf16[2,64,3264]{2,1,0:T(8,128)(2,1)S(1)}, u32[]{:S(2)}, u32[]{:S(2)}) collective-permute-start(bf16[2,64,3264]{2,1,0:T(8,128)(2,1)S(1)} %collective-permute-done.11.refs_3_), channel_id=1, source_target_pairs={{0,1},{1,2},{2,3},{3,4},{4,5},{5,6},{6,7},{8,9},{9,10},{10,11},{11... | collective-permute-start | bytes 2506760 | tf_op jit(solution)/shard_map/ppermute | solution.py:25
  118.2 22.0 %collective-permute-start.13 = (bf16[2,64,3264]{2,1,0:T(8,128)(2,1)S(1)}, bf16[2,64,3264]{2,1,0:T(8,128)(2,1)S(1)}, u32[]{:S(2)}, u32[]{:S(2)}) collective-permute-start(bf16[2,64,3264]{2,1,0:T(8,128)(2,1)S(1)} %collective-permute-done.11.refs_3_), channel_id=1, source_target_pairs={{2,0},{10,8},{18,16},{26,24}} | collective-permute-start | bytes 2506760 | tf_op jit(solution)/shard_map/ppermute | solution.py:32
  119.0 24.3 %copy-start = (s32[40]{0:T(128)S(1)}, s32[40]{0:T(128)}, u32[]{:S(2)}) copy-start(s32[40]{0:T(128)} %sizes.5) | copy-start | bytes 484
  119.1 24.3 %copy-start.1 = (bf16[5,1,4,96,96]{4,3,2,1,0:T(8,128)(2,1)S(1)}, bf16[5,1,4,96,96]{4,3,2,1,0:T(8,128)(2,1)}, u32[]{:S(2)}) copy-start(bf16[5,1,4,96,96]{4,3,2,1,0:T(8,128)(2,1)} %refs_7_.3) | copy-start | bytes 1105924
  119.1 24.2 %collective-permute-start.22 = (bf16[2,64,3264]{2,1,0:T(8,128)(2,1)S(1)}, bf16[2,64,3264]{2,1,0:T(8,128)(2,1)S(1)}, u32[]{:S(2)}, u32[]{:S(2)}) collective-permute-start(bf16[2,64,3264]{2,1,0:T(8,128)(2,1)S(1)} %broadcast_select_fusion), channel_id=1, source_target_pairs={{0,4},{1,2},{2,3},{4,5},{5,6},{6,7},{8,12},{9,10},{10,11},{12,13},... | collective-permute-start | bytes 2506760 | tf_op jit(solution)/shard_map/ppermute | solution.py:35
  137.7 19.7 %collective-permute-start.16 = (bf16[1,64,3264]{2,1,0:T(8,128)(2,1)S(1)}, bf16[1,64,3264]{2,1,0:T(8,128)(2,1)S(1)}, u32[]{:S(2)}, u32[]{:S(2)}) collective-permute-start(bf16[1,64,3264]{2,1,0:T(8,128)(2,1)S(1)} %collective-permute-done.15.refs_2_), channel_id=1, source_target_pairs={{0,1},{1,2},{2,3},{3,4},{4,5},{5,6},{6,7},{8,9},{9,10},{10,11},{11... | collective-permute-start | bytes 1253384 | tf_op jit(solution)/shard_map/ppermute | solution.py:25
  140.3 17.1 %collective-permute-start.14 = (bf16[2,64,3264]{2,1,0:T(8,128)(2,1)S(1)}, bf16[2,64,3264]{2,1,0:T(8,128)(2,1)S(1)}, u32[]{:S(2)}, u32[]{:S(2)}) collective-permute-start(bf16[2,64,3264]{2,1,0:T(8,128)(2,1)S(1)} %broadcast_select_fusion.1), channel_id=1, source_target_pairs={{0,4},{1,2},{2,3},{4,5},{5,6},{6,7},{8,12},{9,10},{10,11},{12,13},... | collective-permute-start | bytes 2506760 | tf_op jit(solution)/shard_map/ppermute | solution.py:35
